TPU v7x, 32 devices: a whole 2x2x4 slice. The times are simulated.
32 devices in a mesh: grp: 2 (over y), gx: 8 (over z, x), gy: 2 (over core).
Axes of the slice: x: 2, y: 2, z: 4, core: 2. Of those that a mesh axis runs over, the one named last changes fastest.
Arguments:
- images: bfloat16 [8, 1024, 2048], P('grp', 'gx', 'gy'), parts along dimension 0, may hold values from 0.049804688 to 5
- weights: bfloat16 [4, 4, 3, 64, 1024], P(None, None, None, None, 'gx'), may hold values from 3.886223e-05 to 0.0390625
- crossings: int32 [4, 4, 8, 3], P(None, None, 'gx'), may hold values from 0 to 3, as said below
- counts: int32 [4, 4, 8], P(None, None, 'gx'), may hold values from 2 to 3, as said below
Outputs:
- smoothed: float32 [8, 1024, 2048], P('grp', 'gx', 'gy'), parts along dimension 0
There are 2 independent parts, one for each index of `grp`. A program takes and returns all parts, laid end to end along the dimension named above; an argument that names none is the same for every part. Nothing has to cross between parts.
Inputs may be any that keep to these rules, and one draw needn't show every extreme that they name: `crossings`: each list names 3 different window blocks in rising order. Only the first counts[c, z, i] entries of a list are crossed; the remaining entries are not used.
All inputs are finite; a program needn't handle non-finite values.
Results may differ from a plain program's by a relative error of at most 0.0003.
Values may be sent and summed in bfloat16 or wider, within the bound.
A program may use at most 64 MiB of HBM per device.

v0:
```python
import jax
import jax.numpy as jnp
from jax import lax
from jax.sharding import PartitionSpec as P

PASSES = 3


def extended(block, sides, width):
    for axis, dim in sides:
        count = lax.axis_size(axis)
        forward = [(i, i + 1) for i in range(count - 1)]
        backward = [(target, source) for source, target in forward]
        low = lax.ppermute(
            lax.slice_in_dim(block, block.shape[dim] - width, None, axis=dim), axis, forward
        )
        high = lax.ppermute(lax.slice_in_dim(block, 0, width, axis=dim), axis, backward)
        block = jnp.concatenate([low, block, high], axis=dim)
    return block


def binomial(framed):
    padded_depth = jnp.pad(framed, ((1, 1), (0, 0), (0, 0)))
    along_z = 0.25 * padded_depth[:-2] + 0.5 * padded_depth[1:-1] + 0.25 * padded_depth[2:]
    along_x = 0.25 * along_z[:, :-2] + 0.5 * along_z[:, 1:-1] + 0.25 * along_z[:, 2:]
    return 0.25 * along_x[:, :, :-2] + 0.5 * along_x[:, :, 1:-1] + 0.25 * along_x[:, :, 2:]


def per_device(images, weights, crossings, counts):
    camera_count = images.shape[0]
    row_count = images.shape[1]
    col_count = images.shape[2]
    slot_count = weights.shape[2]
    block_rows = weights.shape[3]
    window_blocks = row_count // block_rows + 2
    active = jnp.arange(slot_count)[None, None, :] < counts[:, :, 0][:, :, None]
    window = extended(images, (("gx", 1),), block_rows)
    product = None
    for camera in range(camera_count):
        framed = window[camera]
        masked = weights[camera] * active[camera][:, :, None, None].astype(jnp.bfloat16)
        stacked = framed.reshape(window_blocks, block_rows, col_count)
        chosen = stacked[crossings[camera, :, 0, :]]
        projection = jnp.einsum(
            "zksx,zksy->zxy", masked, chosen, preferred_element_type=jnp.float32
        )
        if camera == 0:
            product = projection
        else:
            product = product * projection
    smoothed = product
    for pass_index in range(PASSES):
        framed = extended(smoothed, (("gx", 1), ("gy", 2)), 1)
        smoothed = binomial(framed)
    return smoothed


def solution(mesh):
    in_specs = (
        P("grp", "gx", "gy"),
        P(None, None, None, None, "gx"),
        P(None, None, "gx", None),
        P(None, None, "gx"),
    )
    out_specs = P("grp", "gx", "gy")
    return jax.shard_map(
        per_device, mesh=mesh, in_specs=in_specs, out_specs=out_specs, check_vma=False
    )
```

profile of v0, /device:TPU:0, one launch (start us, length us, event | category | flops | bytes accessed | tf_op | source)
XLA Modules:
  0.0 118.8 jit_solution(12153176477827575590)
XLA Ops:
  0.0 1.4 %fusion.46 = (bf16[4,64,1024]{2,1,0:T(8,128)(2,1)S(1)}, bf16[4,64,1024]{2,1,0:T(8,128)(2,1)S(1)}) fusion(bf16[4,128,1024]{2,1,0:T(8,128)(2,1)} %param.4), kind=kLoop, calls=%fused_computation.100 | loop fusion | bytes 2097152 | tf_op jit(solution)/shard_map/slice | solution.py:17
  1.4 4.9 %collective-permute-start = (bf16[4,64,1024]{2,1,0:T(8,128)(2,1)S(1)}, bf16[4,64,1024]{2,1,0:T(8,128)(2,1)S(1)}, u32[]{:S(2)}, u32[]{:S(2)}) collective-permute-start(bf16[4,64,1024]{2,1,0:T(8,128)(2,1)S(1)} %get-tuple-element.22), channel_id=1, source_target_pairs={{0,2},{2,4},{4,6},{6,8},{8,10},{10,12},{12,14},{1,3},{3,5},{5,7},{... | collective-permute-start | bytes 1572872 | tf_op jit(solution)/shard_map/ppermute | solution.py:14
  6.3 1.3 %collective-permute-start.1 = (bf16[4,64,1024]{2,1,0:T(8,128)(2,1)S(1)}, bf16[4,64,1024]{2,1,0:T(8,128)(2,1)S(1)}, u32[]{:S(2)}, u32[]{:S(2)}) collective-permute-start(bf16[4,64,1024]{2,1,0:T(8,128)(2,1)S(1)} %get-tuple-element.21), channel_id=1, source_target_pairs={{2,0},{4,2},{6,4},{8,6},{10,8},{12,10},{14,12},{3,1},{5,3},{7,5},{... | collective-permute-start | bytes 1572872 | tf_op jit(solution)/shard_map/ppermute | solution.py:17
  7.6 0.7 compare_select_fusion
  9.1 0.8 iota_compare_fusion
  9.8 18.8 %collective-permute-done = bf16[4,64,1024]{2,1,0:T(8,128)(2,1)S(1)} collective-permute-done((bf16[4,64,1024]{2,1,0:T(8,128)(2,1)S(1)}, bf16[4,64,1024]{2,1,0:T(8,128)(2,1)S(1)}, u32[]{:S(2)}, u32[]{:S(2)}) %collective-permute-start) | collective-permute-done | bytes 524320 | tf_op jit(solution)/shard_map/ppermute | solution.py:14
  28.8 0.2 fusion.45
  29.0 1.8 %gather_fusion.1 = bf16[12,64,1024]{2,1,0:T(8,128)(2,1)} fusion(bf16[4,64,1024]{2,1,0:T(8,128)(2,1)S(1)} %bitcast.69, s32[1024]{0:T(1024)S(1)} %get-tuple-element.33), kind=kCustom, calls=%fused_computation.1 | custom fusion | bytes 3145776 | tf_op jit(solution)/shard_map/gather | solution.py:43
  30.9 1.9 %gather_fusion = bf16[12,64,1024]{2,1,0:T(8,128)(2,1)} fusion(bf16[4,64,1024]{2,1,0:T(8,128)(2,1)S(1)} %bitcast.68, s32[1024]{0:T(1024)S(1)} %get-tuple-element.34), kind=kCustom, calls=%fused_computation | custom fusion | bytes 3145776 | tf_op jit(solution)/shard_map/gather | solution.py:43
  32.8 2.4 %fusion.25 = f32[4,128,1024,1]{2,1,3,0:T(8,128)S(1)} fusion(bf16[4,3,64,1024]{3,2,1,0:T(8,128)(2,1)} %bitcast.70, bf16[4,4,3,64,128]{4,3,2,1,0:T(8,128)(2,1)} %param.5, bf16[4,3]{1,0:T(4,128)(2,1)S(1)} %get-tuple-element.29), kind=kOutput, calls=%fused_computation.62 | convolution fusion | flops 201424896 | bytes 3866648 | tf_op jit(solution)/shard_map/zksx,zksy->zxy/dot_general | solution.py:44
  35.2 3.0 %fusion.26 = f32[4,128,1024,1]{2,1,3,0:T(8,128)} fusion(bf16[4,3,64,1024]{3,2,1,0:T(8,128)(2,1)S(1)} %bitcast.71, bf16[4,4,3,64,128]{4,3,2,1,0:T(8,128)(2,1)} %param.5, bf16[4,3]{1,0:T(4,128)(2,1)S(1)} %get-tuple-element.30), kind=kOutput, calls=%fused_computation.64 | convolution fusion | flops 201424896 | bytes 3866648 | tf_op jit(solution)/shard_map/zksx,zksy->zxy/dot_general | solution.py:44
  38.2 1.8 %gather_fusion.2 = bf16[12,64,1024]{2,1,0:T(8,128)(2,1)} fusion(bf16[4,64,1024]{2,1,0:T(8,128)(2,1)S(1)} %bitcast.67, s32[1024]{0:T(1024)S(1)} %get-tuple-element.32), kind=kCustom, calls=%fused_computation.2 | custom fusion | bytes 3145776 | tf_op jit(solution)/shard_map/gather | solution.py:43
  40.1 3.6 %fusion.24 = f32[4,128,1024,1]{2,1,3,0:T(8,128)} fusion(bf16[4,3,64,1024]{3,2,1,0:T(8,128)(2,1)} %bitcast.72, bf16[4,4,3,64,128]{4,3,2,1,0:T(8,128)(2,1)} %param.5, bf16[4,3]{1,0:T(4,128)(2,1)S(1)} %get-tuple-element.28), kind=kOutput, calls=%fused_computation.60 | convolution fusion | flops 201424896 | bytes 3866648 | tf_op jit(solution)/shard_map/zksx,zksy->zxy/dot_general | solution.py:44
  43.7 1.8 %gather_fusion.3 = bf16[12,64,1024]{2,1,0:T(8,128)(2,1)} fusion(bf16[4,64,1024]{2,1,0:T(8,128)(2,1)S(1)} %bitcast.66, s32[1024]{0:T(1024)S(1)} %get-tuple-element.31), kind=kCustom, calls=%fused_computation.3 | custom fusion | bytes 3145776 | tf_op jit(solution)/shard_map/gather | solution.py:43
  45.5 3.6 %bitcast_multiply_fusion = f32[4,128,1024]{2,1,0:T(8,128)S(1)} fusion(f32[4,128,1024,1]{2,1,3,0:T(8,128)} %fusion.24, f32[4,128,1024,1]{2,1,3,0:T(8,128)S(1)} %fusion.25, f32[4,128,1024,1]{2,1,3,0:T(8,128)} %fusion.26, bf16[4,3,64,1024]{3,2,1,0:T(8,128)(2,1)} %bitcast.65, bf16[4,4,3,64,128]{4,3,2,1,0:T(8,128)(2,1)} %param.5, ...), kind=kOutput, calls=%fused_computation.55 | convolution fusion | flops 202997760 | bytes 10158104 | tf_op jit(solution)/shard_map/zksx,zksy->zxy/dot_general | solution.py:44
  49.1 4.4 %collective-permute-start.2 = (f32[4,1,1024]{2,1,0:T(1,128)S(1)}, f32[4,1,1024]{2,1,0:T(1,128)S(1)}, u32[]{:S(2)}, u32[]{:S(2)}) collective-permute-start(f32[4,1,1024]{2,1,0:T(1,128)S(1)} %get-tuple-element.15), channel_id=1, source_target_pairs={{0,2},{2,4},{4,6},{6,8},{8,10},{10,12},{12,14},{1,3},{3,5},{5,7},{... | collective-permute-start | bytes 49160 | tf_op jit(solution)/shard_map/ppermute | solution.py:14
  53.5 1.3 %collective-permute-start.3 = (f32[4,1,1024]{2,1,0:T(1,128)S(1)}, f32[4,1,1024]{2,1,0:T(1,128)S(1)}, u32[]{:S(2)}, u32[]{:S(2)}) collective-permute-start(f32[4,1,1024]{2,1,0:T(1,128)S(1)} %get-tuple-element.16), channel_id=1, source_target_pairs={{2,0},{4,2},{6,4},{8,6},{10,8},{12,10},{14,12},{3,1},{5,3},{7,5},{... | collective-permute-start | bytes 49160 | tf_op jit(solution)/shard_map/ppermute | solution.py:17
  54.9 4.5 %collective-permute-done.3 = f32[4,1,1024]{2,1,0:T(1,128)S(1)} collective-permute-done((f32[4,1,1024]{2,1,0:T(1,128)S(1)}, f32[4,1,1024]{2,1,0:T(1,128)S(1)}, u32[]{:S(2)}, u32[]{:S(2)}) %collective-permute-start.3) | collective-permute-done | bytes 16416 | tf_op jit(solution)/shard_map/ppermute | solution.py:17
  59.4 0.3 pad_maximum_fusion
  59.9 1.3 %collective-permute-start.4 = (f32[4,130,1]{2,1,0:T(8,128)S(1)}, f32[4,130,1]{2,1,0:T(8,128)S(1)}, u32[]{:S(2)}, u32[]{:S(2)}) collective-permute-start(f32[4,130,1]{2,1,0:T(8,128)S(1)} %get-tuple-element.10), channel_id=1, source_target_pairs={{0,1},{2,3},{4,5},{6,7},{8,9},{10,11},{12,13},{14,15},{16,17},{18,... | collective-permute-start | bytes 6248 | tf_op jit(solution)/shard_map/ppermute | solution.py:14
  61.2 1.3 %collective-permute-start.5 = (f32[4,130,1]{2,1,0:T(8,128)S(1)}, f32[4,130,1]{2,1,0:T(8,128)S(1)}, u32[]{:S(2)}, u32[]{:S(2)}) collective-permute-start(f32[4,130,1]{2,1,0:T(8,128)S(1)} %get-tuple-element.9), channel_id=1, source_target_pairs={{1,0},{3,2},{5,4},{7,6},{9,8},{11,10},{13,12},{15,14},{17,16},{19,... | collective-permute-start | bytes 6248 | tf_op jit(solution)/shard_map/ppermute | solution.py:17
  62.5 2.1 %collective-permute-done.5 = f32[4,130,1]{2,1,0:T(8,128)S(1)} collective-permute-done((f32[4,130,1]{2,1,0:T(8,128)S(1)}, f32[4,130,1]{2,1,0:T(8,128)S(1)}, u32[]{:S(2)}, u32[]{:S(2)}) %collective-permute-start.5) | collective-permute-done | bytes 2112 | tf_op jit(solution)/shard_map/ppermute | solution.py:17
  64.7 2.7 %concatenate.23 = f32[4,130,1026]{2,1,0:T(8,128)} concatenate(f32[4,130,1]{2,1,0:T(8,128)S(1)} %collective-permute-done.4, f32[4,130,1024]{2,1,0:T(8,128)S(1)} %pad_maximum_fusion, f32[4,130,1]{2,1,0:T(8,128)S(1)} %collective-permute-done.5), dimensions={2} | concatenate | bytes 4268160 | tf_op jit(solution)/shard_map/concatenate | solution.py:18
  67.4 3.2 %fusion.2 = f32[4,130,1026]{2,1,0:T(8,128)S(1)} fusion(f32[4,130,1026]{2,1,0:T(8,128)} %concatenate.23), kind=kLoop, calls=%fused_computation.12 | loop fusion | flops 2667600 | bytes 4268160 | tf_op jit(solution)/shard_map/add | solution.py:24
  70.6 0.7 fusion.16
  71.3 1.1 fusion.22
  72.5 4.8 %collective-permute-start.6 = (f32[4,1,1024]{2,1,0:T(1,128)S(1)}, f32[4,1,1024]{2,1,0:T(1,128)S(1)}, u32[]{:S(2)}, u32[]{:S(2)}) collective-permute-start(f32[4,1,1024]{2,1,0:T(1,128)S(1)} %get-tuple-element.13), channel_id=1, source_target_pairs={{0,2},{2,4},{4,6},{6,8},{8,10},{10,12},{12,14},{1,3},{3,5},{5,7},{... | collective-permute-start | bytes 49160 | tf_op jit(solution)/shard_map/ppermute | solution.py:14
  77.3 1.3 %collective-permute-start.7 = (f32[4,1,1024]{2,1,0:T(1,128)S(1)}, f32[4,1,1024]{2,1,0:T(1,128)S(1)}, u32[]{:S(2)}, u32[]{:S(2)}) collective-permute-start(f32[4,1,1024]{2,1,0:T(1,128)S(1)} %get-tuple-element.14), channel_id=1, source_target_pairs={{2,0},{4,2},{6,4},{8,6},{10,8},{12,10},{14,12},{3,1},{5,3},{7,5},{... | collective-permute-start | bytes 49160 | tf_op jit(solution)/shard_map/ppermute | solution.py:17
  78.7 4.2 %collective-permute-done.7 = f32[4,1,1024]{2,1,0:T(1,128)S(1)} collective-permute-done((f32[4,1,1024]{2,1,0:T(1,128)S(1)}, f32[4,1,1024]{2,1,0:T(1,128)S(1)}, u32[]{:S(2)}, u32[]{:S(2)}) %collective-permute-start.7) | collective-permute-done | bytes 16416 | tf_op jit(solution)/shard_map/ppermute | solution.py:17
  82.9 0.3 pad_maximum_fusion.1
  83.4 1.3 %collective-permute-start.8 = (f32[4,130,1]{2,1,0:T(8,128)S(1)}, f32[4,130,1]{2,1,0:T(8,128)S(1)}, u32[]{:S(2)}, u32[]{:S(2)}) collective-permute-start(f32[4,130,1]{2,1,0:T(8,128)S(1)} %get-tuple-element.8), channel_id=1, source_target_pairs={{0,1},{2,3},{4,5},{6,7},{8,9},{10,11},{12,13},{14,15},{16,17},{18,... | collective-permute-start | bytes 6248 | tf_op jit(solution)/shard_map/ppermute | solution.py:14
  84.7 1.3 %collective-permute-start.9 = (f32[4,130,1]{2,1,0:T(8,128)S(1)}, f32[4,130,1]{2,1,0:T(8,128)S(1)}, u32[]{:S(2)}, u32[]{:S(2)}) collective-permute-start(f32[4,130,1]{2,1,0:T(8,128)S(1)} %get-tuple-element.7), channel_id=1, source_target_pairs={{1,0},{3,2},{5,4},{7,6},{9,8},{11,10},{13,12},{15,14},{17,16},{19,... | collective-permute-start | bytes 6248 | tf_op jit(solution)/shard_map/ppermute | solution.py:17
  86.0 2.1 %collective-permute-done.9 = f32[4,130,1]{2,1,0:T(8,128)S(1)} collective-permute-done((f32[4,130,1]{2,1,0:T(8,128)S(1)}, f32[4,130,1]{2,1,0:T(8,128)S(1)}, u32[]{:S(2)}, u32[]{:S(2)}) %collective-permute-start.9) | collective-permute-done | bytes 2112 | tf_op jit(solution)/shard_map/ppermute | solution.py:17
  88.1 2.7 %concatenate.25 = f32[4,130,1026]{2,1,0:T(8,128)} concatenate(f32[4,130,1]{2,1,0:T(8,128)S(1)} %collective-permute-done.8, f32[4,130,1024]{2,1,0:T(8,128)S(1)} %pad_maximum_fusion.1, f32[4,130,1]{2,1,0:T(8,128)S(1)} %collective-permute-done.9), dimensions={2} | concatenate | bytes 4268160 | tf_op jit(solution)/shard_map/concatenate | solution.py:18
  90.8 3.2 %fusion.6 = f32[4,130,1026]{2,1,0:T(8,128)S(1)} fusion(f32[4,130,1026]{2,1,0:T(8,128)} %concatenate.25), kind=kLoop, calls=%fused_computation.16 | loop fusion | flops 2667600 | bytes 4268160 | tf_op jit(solution)/shard_map/add | solution.py:24
  94.1 0.7 fusion.14
  94.8 1.1 fusion.20
  95.9 2.9 %collective-permute-start.10 = (f32[4,1,1024]{2,1,0:T(1,128)S(1)}, f32[4,1,1024]{2,1,0:T(1,128)S(1)}, u32[]{:S(2)}, u32[]{:S(2)}) collective-permute-start(f32[4,1,1024]{2,1,0:T(1,128)S(1)} %get-tuple-element.11), channel_id=1, source_target_pairs={{0,2},{2,4},{4,6},{6,8},{8,10},{10,12},{12,14},{1,3},{3,5},{5,7},{... | collective-permute-start | bytes 49160 | tf_op jit(solution)/shard_map/ppermute | solution.py:14
  98.9 1.3 %collective-permute-start.11 = (f32[4,1,1024]{2,1,0:T(1,128)S(1)}, f32[4,1,1024]{2,1,0:T(1,128)S(1)}, u32[]{:S(2)}, u32[]{:S(2)}) collective-permute-start(f32[4,1,1024]{2,1,0:T(1,128)S(1)} %get-tuple-element.12), channel_id=1, source_target_pairs={{2,0},{4,2},{6,4},{8,6},{10,8},{12,10},{14,12},{3,1},{5,3},{7,5},{... | collective-permute-start | bytes 49160 | tf_op jit(solution)/shard_map/ppermute | solution.py:17
  100.3 4.2 %collective-permute-done.11 = f32[4,1,1024]{2,1,0:T(1,128)S(1)} collective-permute-done((f32[4,1,1024]{2,1,0:T(1,128)S(1)}, f32[4,1,1024]{2,1,0:T(1,128)S(1)}, u32[]{:S(2)}, u32[]{:S(2)}) %collective-permute-start.11) | collective-permute-done | bytes 16416 | tf_op jit(solution)/shard_map/ppermute | solution.py:17
  104.5 0.3 pad_maximum_fusion.2
  105.0 1.3 %collective-permute-start.12 = (f32[4,130,1]{2,1,0:T(8,128)S(1)}, f32[4,130,1]{2,1,0:T(8,128)S(1)}, u32[]{:S(2)}, u32[]{:S(2)}) collective-permute-start(f32[4,130,1]{2,1,0:T(8,128)S(1)} %get-tuple-element.6), channel_id=1, source_target_pairs={{0,1},{2,3},{4,5},{6,7},{8,9},{10,11},{12,13},{14,15},{16,17},{18,... | collective-permute-start | bytes 6248 | tf_op jit(solution)/shard_map/ppermute | solution.py:14
  106.3 1.5 %collective-permute-start.13 = (f32[4,130,1]{2,1,0:T(8,128)S(1)}, f32[4,130,1]{2,1,0:T(8,128)S(1)}, u32[]{:S(2)}, u32[]{:S(2)}) collective-permute-start(f32[4,130,1]{2,1,0:T(8,128)S(1)} %get-tuple-element.5), channel_id=1, source_target_pairs={{1,0},{3,2},{5,4},{7,6},{9,8},{11,10},{13,12},{15,14},{17,16},{19,... | collective-permute-start | bytes 6248 | tf_op jit(solution)/shard_map/ppermute | solution.py:17
  107.8 2.0 %collective-permute-done.13 = f32[4,130,1]{2,1,0:T(8,128)S(1)} collective-permute-done((f32[4,130,1]{2,1,0:T(8,128)S(1)}, f32[4,130,1]{2,1,0:T(8,128)S(1)}, u32[]{:S(2)}, u32[]{:S(2)}) %collective-permute-start.13) | collective-permute-done | bytes 2112 | tf_op jit(solution)/shard_map/ppermute | solution.py:17
  109.7 2.7 %concatenate.27 = f32[4,130,1026]{2,1,0:T(8,128)} concatenate(f32[4,130,1]{2,1,0:T(8,128)S(1)} %collective-permute-done.12, f32[4,130,1024]{2,1,0:T(8,128)S(1)} %pad_maximum_fusion.2, f32[4,130,1]{2,1,0:T(8,128)S(1)} %collective-permute-done.13), dimensions={2} | concatenate | bytes 4268160 | tf_op jit(solution)/shard_map/concatenate | solution.py:18
  112.4 3.2 %fusion.10 = f32[4,130,1026]{2,1,0:T(8,128)S(1)} fusion(f32[4,130,1026]{2,1,0:T(8,128)} %concatenate.27), kind=kLoop, calls=%fused_computation.20 | loop fusion | flops 2667600 | bytes 4268160 | tf_op jit(solution)/shard_map/add | solution.py:24
  115.7 0.7 fusion.12
  116.4 2.5 %fusion.18 = f32[4,128,1024]{2,1,0:T(8,128)} fusion(f32[4,128,1026]{2,1,0:T(8,128)S(1)} %fusion.12), kind=kLoop, calls=%fused_computation.41 | loop fusion | flops 2621440 | bytes 8388608 | tf_op jit(solution)/shard_map/add | solution.py:26
  (31 shorter events, 1.8 us)
Async XLA Ops:
  0.0 28.7 %copy-start.1 = (bf16[4,128,1024]{2,1,0:T(8,128)(2,1)S(1)}, bf16[4,128,1024]{2,1,0:T(8,128)(2,1)}, u32[]{:S(2)}) copy-start(bf16[4,128,1024]{2,1,0:T(8,128)(2,1)} %param.4) | copy-start | bytes 3145732
  1.4 27.2 %collective-permute-start = (bf16[4,64,1024]{2,1,0:T(8,128)(2,1)S(1)}, bf16[4,64,1024]{2,1,0:T(8,128)(2,1)S(1)}, u32[]{:S(2)}, u32[]{:S(2)}) collective-permute-start(bf16[4,64,1024]{2,1,0:T(8,128)(2,1)S(1)} %get-tuple-element.22), channel_id=1, source_target_pairs={{0,2},{2,4},{4,6},{6,8},{8,10},{10,12},{12,14},{1,3},{3,5},{5,7},{... | collective-permute-start | bytes 1572872 | tf_op jit(solution)/shard_map/ppermute | solution.py:14
  6.3 22.5 %collective-permute-start.1 = (bf16[4,64,1024]{2,1,0:T(8,128)(2,1)S(1)}, bf16[4,64,1024]{2,1,0:T(8,128)(2,1)S(1)}, u32[]{:S(2)}, u32[]{:S(2)}) collective-permute-start(bf16[4,64,1024]{2,1,0:T(8,128)(2,1)S(1)} %get-tuple-element.21), channel_id=1, source_target_pairs={{2,0},{4,2},{6,4},{8,6},{10,8},{12,10},{14,12},{3,1},{5,3},{7,5},{... | collective-permute-start | bytes 1572872 | tf_op jit(solution)/shard_map/ppermute | solution.py:17
  32.8 2.4 %copy-start = (bf16[12,64,1024]{2,1,0:T(8,128)(2,1)S(1)}, bf16[12,64,1024]{2,1,0:T(8,128)(2,1)}, u32[]{:S(2)}) copy-start(bf16[12,64,1024]{2,1,0:T(8,128)(2,1)} %gather_fusion) | copy-start | bytes 4718596
  49.1 5.8 %collective-permute-start.2 = (f32[4,1,1024]{2,1,0:T(1,128)S(1)}, f32[4,1,1024]{2,1,0:T(1,128)S(1)}, u32[]{:S(2)}, u32[]{:S(2)}) collective-permute-start(f32[4,1,1024]{2,1,0:T(1,128)S(1)} %get-tuple-element.15), channel_id=1, source_target_pairs={{0,2},{2,4},{4,6},{6,8},{8,10},{10,12},{12,14},{1,3},{3,5},{5,7},{... | collective-permute-start | bytes 49160 | tf_op jit(solution)/shard_map/ppermute | solution.py:14
  53.5 5.9 %collective-permute-start.3 = (f32[4,1,1024]{2,1,0:T(1,128)S(1)}, f32[4,1,1024]{2,1,0:T(1,128)S(1)}, u32[]{:S(2)}, u32[]{:S(2)}) collective-permute-start(f32[4,1,1024]{2,1,0:T(1,128)S(1)} %get-tuple-element.16), channel_id=1, source_target_pairs={{2,0},{4,2},{6,4},{8,6},{10,8},{12,10},{14,12},{3,1},{5,3},{7,5},{... | collective-permute-start | bytes 49160 | tf_op jit(solution)/shard_map/ppermute | solution.py:17
  59.9 2.6 %collective-permute-start.4 = (f32[4,130,1]{2,1,0:T(8,128)S(1)}, f32[4,130,1]{2,1,0:T(8,128)S(1)}, u32[]{:S(2)}, u32[]{:S(2)}) collective-permute-start(f32[4,130,1]{2,1,0:T(8,128)S(1)} %get-tuple-element.10), channel_id=1, source_target_pairs={{0,1},{2,3},{4,5},{6,7},{8,9},{10,11},{12,13},{14,15},{16,17},{18,... | collective-permute-start | bytes 6248 | tf_op jit(solution)/shard_map/ppermute | solution.py:14
  61.2 3.5 %collective-permute-start.5 = (f32[4,130,1]{2,1,0:T(8,128)S(1)}, f32[4,130,1]{2,1,0:T(8,128)S(1)}, u32[]{:S(2)}, u32[]{:S(2)}) collective-permute-start(f32[4,130,1]{2,1,0:T(8,128)S(1)} %get-tuple-element.9), channel_id=1, source_target_pairs={{1,0},{3,2},{5,4},{7,6},{9,8},{11,10},{13,12},{15,14},{17,16},{19,... | collective-permute-start | bytes 6248 | tf_op jit(solution)/shard_map/ppermute | solution.py:17
  72.5 6.3 %collective-permute-start.6 = (f32[4,1,1024]{2,1,0:T(1,128)S(1)}, f32[4,1,1024]{2,1,0:T(1,128)S(1)}, u32[]{:S(2)}, u32[]{:S(2)}) collective-permute-start(f32[4,1,1024]{2,1,0:T(1,128)S(1)} %get-tuple-element.13), channel_id=1, source_target_pairs={{0,2},{2,4},{4,6},{6,8},{8,10},{10,12},{12,14},{1,3},{3,5},{5,7},{... | collective-permute-start | bytes 49160 | tf_op jit(solution)/shard_map/ppermute | solution.py:14
  77.3 5.6 %collective-permute-start.7 = (f32[4,1,1024]{2,1,0:T(1,128)S(1)}, f32[4,1,1024]{2,1,0:T(1,128)S(1)}, u32[]{:S(2)}, u32[]{:S(2)}) collective-permute-start(f32[4,1,1024]{2,1,0:T(1,128)S(1)} %get-tuple-element.14), channel_id=1, source_target_pairs={{2,0},{4,2},{6,4},{8,6},{10,8},{12,10},{14,12},{3,1},{5,3},{7,5},{... | collective-permute-start | bytes 49160 | tf_op jit(solution)/shard_map/ppermute | solution.py:17
  83.4 2.6 %collective-permute-start.8 = (f32[4,130,1]{2,1,0:T(8,128)S(1)}, f32[4,130,1]{2,1,0:T(8,128)S(1)}, u32[]{:S(2)}, u32[]{:S(2)}) collective-permute-start(f32[4,130,1]{2,1,0:T(8,128)S(1)} %get-tuple-element.8), channel_id=1, source_target_pairs={{0,1},{2,3},{4,5},{6,7},{8,9},{10,11},{12,13},{14,15},{16,17},{18,... | collective-permute-start | bytes 6248 | tf_op jit(solution)/shard_map/ppermute | solution.py:14
  84.7 3.5 %collective-permute-start.9 = (f32[4,130,1]{2,1,0:T(8,128)S(1)}, f32[4,130,1]{2,1,0:T(8,128)S(1)}, u32[]{:S(2)}, u32[]{:S(2)}) collective-permute-start(f32[4,130,1]{2,1,0:T(8,128)S(1)} %get-tuple-element.7), channel_id=1, source_target_pairs={{1,0},{3,2},{5,4},{7,6},{9,8},{11,10},{13,12},{15,14},{17,16},{19,... | collective-permute-start | bytes 6248 | tf_op jit(solution)/shard_map/ppermute | solution.py:17
  95.9 4.4 %collective-permute-start.10 = (f32[4,1,1024]{2,1,0:T(1,128)S(1)}, f32[4,1,1024]{2,1,0:T(1,128)S(1)}, u32[]{:S(2)}, u32[]{:S(2)}) collective-permute-start(f32[4,1,1024]{2,1,0:T(1,128)S(1)} %get-tuple-element.11), channel_id=1, source_target_pairs={{0,2},{2,4},{4,6},{6,8},{8,10},{10,12},{12,14},{1,3},{3,5},{5,7},{... | collective-permute-start | bytes 49160 | tf_op jit(solution)/shard_map/ppermute | solution.py:14
  98.9 5.6 %collective-permute-start.11 = (f32[4,1,1024]{2,1,0:T(1,128)S(1)}, f32[4,1,1024]{2,1,0:T(1,128)S(1)}, u32[]{:S(2)}, u32[]{:S(2)}) collective-permute-start(f32[4,1,1024]{2,1,0:T(1,128)S(1)} %get-tuple-element.12), channel_id=1, source_target_pairs={{2,0},{4,2},{6,4},{8,6},{10,8},{12,10},{14,12},{3,1},{5,3},{7,5},{... | collective-permute-start | bytes 49160 | tf_op jit(solution)/shard_map/ppermute | solution.py:17
  105.0 2.8 %collective-permute-start.12 = (f32[4,130,1]{2,1,0:T(8,128)S(1)}, f32[4,130,1]{2,1,0:T(8,128)S(1)}, u32[]{:S(2)}, u32[]{:S(2)}) collective-permute-start(f32[4,130,1]{2,1,0:T(8,128)S(1)} %get-tuple-element.6), channel_id=1, source_target_pairs={{0,1},{2,3},{4,5},{6,7},{8,9},{10,11},{12,13},{14,15},{16,17},{18,... | collective-permute-start | bytes 6248 | tf_op jit(solution)/shard_map/ppermute | solution.py:14
  106.3 3.5 %collective-permute-start.13 = (f32[4,130,1]{2,1,0:T(8,128)S(1)}, f32[4,130,1]{2,1,0:T(8,128)S(1)}, u32[]{:S(2)}, u32[]{:S(2)}) collective-permute-start(f32[4,130,1]{2,1,0:T(8,128)S(1)} %get-tuple-element.5), channel_id=1, source_target_pairs={{1,0},{3,2},{5,4},{7,6},{9,8},{11,10},{13,12},{15,14},{17,16},{19,... | collective-permute-start | bytes 6248 | tf_op jit(solution)/shard_map/ppermute | solution.py:17
where the time goes:
time: 120 us; the launch traced here: 119 us
  waiting for transfers between devices  38.4 us (32%)
  starting transfers between devices  30.2 us (25%)
  other arithmetic  18.8 us (16%)
  local copies, waits for them, and re-layouts  18.5 us (15%)
  matrix products  12.7 us (11%)
    ppermute x7, starting transfers between devices, extended(): lax.ppermute(lax.slice_in_dim(block, block.shape[dim] - width, None, axis...  20.9 us
    ppermute x7, waiting for transfers between devices, extended(): lax.ppermute(lax.slice_in_dim(block, block.shape[dim] - width, None, axis...  19.2 us
    ppermute x7, waiting for transfers between devices, extended(): lax.ppermute(lax.slice_in_dim(block, 0, width, axis=dim), axis, backward)  19.2 us
    dot_general x4, matrix products, per_device(): jnp.einsum('zksx,zksy->zxy', masked, chosen, preferred_element_type=jnp.f...  12.7 us
    add x3, other arithmetic, binomial(): 0.25 * padded_depth[:-2] + 0.5 * padded_depth[1:-1]  9.62 us
    ppermute x7, starting transfers between devices, extended(): lax.ppermute(lax.slice_in_dim(block, 0, width, axis=dim), axis, backward)  9.23 us
    concatenate x4, local copies, waits for them, and re-layouts, extended(): block = jnp.concatenate([low, block, high], axis=dim)  8.17 us
    gather x4, local copies, waits for them, and re-layouts, per_device(): chosen = stacked[crossings[camera, :, 0, :]]  7.37 us
  transfers between devices with their start and end apart: 14, of which 10 were waited for; matrix products, arithmetic and copies ran while one was open for 2% of the time, Pallas kernels for 0%

commit v1 on v0

v1 whole, which is shorter than its diff:
```python
import functools

import jax
import jax.numpy as jnp
import numpy as np
from jax import lax
from jax.experimental import pallas as pl
from jax.experimental.pallas import tpu as pltpu
from jax.sharding import PartitionSpec as P

PASSES = 3
CHUNKS = 4
LANES = 128
BF = jnp.bfloat16
F32 = jnp.float32


def taps(distance):
    distance = jnp.abs(distance)
    value = jnp.where(distance == 0, 20.0, 0.0)
    for far, weight in ((1, 15.0), (2, 6.0), (3, 1.0)):
        value = jnp.where(distance == far, weight, value)
    return value.astype(F32)


def iota(shape, dim):
    return lax.broadcasted_iota(jnp.int32, shape, dim)


def layer_matrix(depth):
    step = 0.5 * np.eye(depth) + 0.25 * (np.eye(depth, k=1) + np.eye(depth, k=-1))
    return np.linalg.matrix_power(step, PASSES)


def split(value):
    high = value.astype(BF)
    return high, (value - high.astype(F32)).astype(BF)


def dot(a, b):
    return jnp.dot(a, b, preferred_element_type=F32)


def kernel(dims, lists, counts, images, weights, out,
           window, stack, spread, prod, part, field, done, out_stage, across, along, edge, pick, beside,
           outbox, inbox, img_send, img_recv, halo_send, halo_recv, seam_sem, local_sem, out_sem):
    cams, depth, slots, sub, tile, cols, n_gx = dims
    width = cols // CHUNKS
    blocks = tile // sub + 2
    gx, gy = lax.axis_index("gx"), lax.axis_index("gy")
    has_lo, has_hi = gx > 0, gx < n_gx - 1
    first = jnp.where(has_lo, 0.0, 1.0).astype(F32)
    last = jnp.where(has_hi, 0.0, 1.0).astype(F32)
    lo, hi, peer = {"gx": gx - 1}, {"gx": gx + 1}, {"gy": 1 - gy}

    def offset(j):
        return pl.multiple_of(jnp.where(gy == 0, (CHUNKS - 1 - j) * width, j * width), width)

    barrier = pltpu.get_barrier_semaphore()

    @pl.when(has_lo)
    def _():
        pl.semaphore_signal(barrier, inc=1, device_id=lo, device_id_type=pl.DeviceIdType.MESH)

    @pl.when(has_hi)
    def _():
        pl.semaphore_signal(barrier, inc=1, device_id=hi, device_id_type=pl.DeviceIdType.MESH)

    pl.semaphore_signal(barrier, inc=1, device_id=peer, device_id_type=pl.DeviceIdType.MESH)

    load_w = pltpu.make_async_copy(weights, stack, local_sem.at[0])
    load_i = pltpu.make_async_copy(images, window.at[:, pl.ds(sub, tile), :], local_sem.at[1])
    load_w.start()
    load_i.start()

    pl.semaphore_wait(barrier, 1 + jnp.where(has_lo, 1, 0) + jnp.where(has_hi, 1, 0))

    def remote(src, dst, send, recv, where):
        return pltpu.make_async_remote_copy(
            src_ref=src, dst_ref=dst, send_sem=send, recv_sem=recv,
            device_id=where, device_id_type=pl.DeviceIdType.MESH)

    def image_copy(j, up):
        cut = pl.ds(offset(j), width)
        if up:
            return remote(images.at[:, pl.ds(tile - sub, sub), cut], window.at[:, pl.ds(0, sub), cut],
                          img_send.at[0, j], img_recv.at[0, j], hi)
        return remote(images.at[:, pl.ds(0, sub), cut], window.at[:, pl.ds(tile + sub, sub), cut],
                      img_send.at[1, j], img_recv.at[1, j], lo)

    def halo_copy(j, up):
        if up:
            return remote(outbox.at[j, pl.ds(16, 16)], inbox.at[j, pl.ds(0, 16)],
                          halo_send.at[0, j], halo_recv.at[0, j], hi)
        return remote(outbox.at[j, pl.ds(0, 16)], inbox.at[j, pl.ds(16, 16)],
                      halo_send.at[1, j], halo_recv.at[1, j], lo)

    def both(make, send, recv):
        def act(copy, start, finish):
            if start:
                copy.start()
            if finish == "send":
                copy.wait_send()
            if finish == "recv":
                copy.wait_recv()

        if send is not None:
            pl.when(has_hi)(lambda: act(make(True), send == "start", send))
            pl.when(has_lo)(lambda: act(make(False), send == "start", send))
        if recv is not None:
            pl.when(has_lo)(lambda: act(make(True), False, "recv"))
            pl.when(has_hi)(lambda: act(make(False), False, "recv"))

    for j in range(CHUNKS):
        both(functools.partial(image_copy, j), "start", None)

    @pl.when(jnp.logical_not(has_lo))
    def _():
        window[:, pl.ds(0, sub), :] = jnp.zeros((cams, sub, cols), BF)
        inbox[:, pl.ds(0, 16), :] = jnp.zeros((CHUNKS, 16, width), BF)

    @pl.when(jnp.logical_not(has_hi))
    def _():
        window[:, pl.ds(tile + sub, sub), :] = jnp.zeros((cams, sub, cols), BF)
        inbox[:, pl.ds(16, 16), :] = jnp.zeros((CHUNKS, 16, width), BF)

    outer = pl.multiple_of(jnp.where(gy == 0, 0, cols + LANES), LANES)
    inner = pl.multiple_of(jnp.where(gy == 0, cols + LANES, 0), LANES)
    field[:, :, pl.ds(outer, LANES)] = jnp.zeros((2, depth * tile, LANES), BF)

    i, k = iota((tile, tile), 0), iota((tile, tile), 1)
    along[...] = ((taps(i - k) - first * taps(i + k + 2) - last * taps(2 * tile - i - k)) / 64).astype(BF)
    r, k = iota((depth * tile, 32), 0), iota((depth * tile, 32), 1)
    q, zz = k % 4, (k // 4) % depth
    place = jnp.where(k < 16, q - 3, tile + q)
    near = jnp.where((q < 3) & (zz == r // tile), taps(r % tile - place), 0.0)
    beside[...] = (near / 64).astype(BF)
    k, r = iota((32, depth * tile), 0), iota((32, depth * tile), 1)
    q, zz = k % 4, (k // 4) % depth
    place = zz * tile + jnp.where(k < 16, q, tile - 3 + q)
    pick[...] = jnp.where((q < 3) & (place == r), 1.0, 0.0).astype(BF)
    a, b = iota((width + 2 * LANES, width), 0) - LANES, iota((width + 2 * LANES, width), 1)
    across[...] = (taps(a - b) / 64).astype(BF)
    mirror = jnp.where(gy == 0, a + b + 2, 2 * width - a - b)
    mirror = jnp.where((a >= 0) & (a < width), mirror, 4)
    edge[...] = ((taps(a - b) - taps(mirror)) / 64).astype(BF)

    load_w.wait()
    for c in range(cams):
        for z in range(depth):
            mats = [stack[c, z, s].astype(F32) for s in range(slots)]
            rows = []
            for w in range(blocks):
                total = None
                for s in range(slots):
                    used = (lists[c, s, 0, z] == w) & (s < counts[c, 0, z])
                    term = mats[s] * jnp.where(used, 1.0, 0.0).astype(F32)
                    total = term if total is None else total + term
                rows.append(total)
            whole = jnp.concatenate(rows, axis=0)
            spread[c, pl.ds(z * tile, tile), :] = jnp.transpose(whole).astype(BF)
    load_i.wait()

    layers = layer_matrix(depth)

    def project(j):
        cut = pl.ds(offset(j), width)
        both(functools.partial(image_copy, j), None, "recv")
        for c in range(cams):
            now = dot(spread[c], window[c, :, cut])
            if c == 0:
                prod[...] = now
            else:
                prod[...] = prod[...] * now
        for z in range(depth):
            total = None
            for s in range(depth):
                if layers[z, s] != 0.0:
                    term = prod[pl.ds(s * tile, tile), :] * float(layers[z, s])
                    total = term if total is None else total + term
            high, low = split(total)
            part[0, pl.ds(z * tile, tile), :] = high
            part[1, pl.ds(z * tile, tile), :] = low
        outbox[j] = dot(pick[...], part[0]).astype(BF)
        both(functools.partial(halo_copy, j), "start", None)
        for z in range(depth):
            rows = pl.ds(z * tile, tile)
            done[j % 2, rows, :] = dot(along[...], part[0, rows, :]) + dot(along[...], part[1, rows, :])

    def finish_x(j):
        both(functools.partial(halo_copy, j), None, "recv")
        high, low = split(done[j % 2] + dot(beside[...], inbox[j]))
        cut = pl.ds(pl.multiple_of(offset(j) + LANES, LANES), width)
        field[0, :, cut] = high
        field[1, :, cut] = low

    mine = pl.multiple_of(jnp.where(gy == 0, cols, LANES), LANES)
    theirs = pl.multiple_of(jnp.where(gy == 0, 0, cols + LANES), LANES)
    seam = remote(field.at[:, :, pl.ds(mine, LANES)], field.at[:, :, pl.ds(theirs, LANES)],
                  seam_sem.at[0], seam_sem.at[1], peer)

    def store(j):
        return pltpu.make_async_copy(
            out_stage.at[j], out.at[:, :, pl.ds(offset(j), width)], out_sem.at[j])

    def finish_y(j):
        if j == 0:
            seam.wait_recv()
        cut = pl.ds(offset(j), width + 2 * LANES)
        mat = (edge if j == CHUNKS - 1 else across)[...]
        full = dot(field[0, :, cut], mat) + dot(field[1, :, cut], mat)
        out_stage[j] = full.reshape(depth, tile, width)
        store(j).start()

    for j in range(CHUNKS):
        project(j)
        if j >= 1:
            finish_x(j - 1)
            if j == 1:
                seam.start()
        if j >= 2:
            finish_y(j - 2)
    finish_x(CHUNKS - 1)
    finish_y(CHUNKS - 2)
    finish_y(CHUNKS - 1)
    for j in range(CHUNKS):
        both(functools.partial(image_copy, j), "send", None)
        both(functools.partial(halo_copy, j), "send", None)
        store(j).wait()
    seam.wait_send()


def per_device(n_gx, images, weights, crossings, counts):
    cams, tile, cols = images.shape
    depth, slots, sub = weights.shape[1:4]
    width, blocks = cols // CHUNKS, tile // sub + 2
    rows = depth * tile
    anywhere = pl.BlockSpec(memory_space=pl.ANY)
    scalars = pl.BlockSpec(memory_space=pltpu.SMEM)
    return pl.pallas_call(
        functools.partial(kernel, (cams, depth, slots, sub, tile, cols, n_gx)),
        out_shape=jax.ShapeDtypeStruct((depth, tile, cols), F32),
        in_specs=[scalars, scalars, anywhere, anywhere],
        out_specs=anywhere,
        scratch_shapes=[
            pltpu.VMEM((cams, blocks * sub, cols), BF),
            pltpu.VMEM(weights.shape, BF),
            pltpu.VMEM((cams, rows, blocks * sub), BF),
            pltpu.VMEM((rows, width), F32),
            pltpu.VMEM((2, rows, width), BF),
            pltpu.VMEM((2, rows, cols + 2 * LANES), BF),
            pltpu.VMEM((2, rows, width), F32),
            pltpu.VMEM((CHUNKS, depth, tile, width), F32),
            pltpu.VMEM((width + 2 * LANES, width), BF),
            pltpu.VMEM((tile, tile), BF),
            pltpu.VMEM((width + 2 * LANES, width), BF),
            pltpu.VMEM((32, rows), BF),
            pltpu.VMEM((rows, 32), BF),
            pltpu.VMEM((CHUNKS, 32, width), BF),
            pltpu.VMEM((CHUNKS, 32, width), BF),
            pltpu.SemaphoreType.DMA((2, CHUNKS)),
            pltpu.SemaphoreType.DMA((2, CHUNKS)),
            pltpu.SemaphoreType.DMA((2, CHUNKS)),
            pltpu.SemaphoreType.DMA((2, CHUNKS)),
            pltpu.SemaphoreType.DMA((2,)),
            pltpu.SemaphoreType.DMA((2,)),
            pltpu.SemaphoreType.DMA((CHUNKS,)),
        ],
        compiler_params=pltpu.CompilerParams(
            collective_id=0, has_side_effects=True, vmem_limit_bytes=60 * 2**20
        ),
    )(
        jnp.transpose(crossings, (0, 3, 2, 1)),
        jnp.transpose(counts, (0, 2, 1)),
        images,
        weights,
    )


def solution(mesh):
    in_specs = (
        P("grp", "gx", "gy"),
        P(None, None, None, None, "gx"),
        P(None, None, "gx", None),
        P(None, None, "gx"),
    )
    return jax.shard_map(
        functools.partial(per_device, mesh.shape["gx"]),
        mesh=mesh, in_specs=in_specs, out_specs=P("grp", "gx", "gy"), check_vma=False
    )
```

time: 120 us -> 40.2 us (0.34)
  waiting for transfers between devices: 38.4 us -> 0 us
  Pallas kernels: 0 us -> 36.9 us
  starting transfers between devices: 30.2 us -> 0 us
  other arithmetic: 18.8 us -> 0 us
  local copies, waits for them, and re-layouts: 18.5 us -> 3.16 us
  matrix products: 12.7 us -> 0 us
    ppermute x14 -> x0, waiting for transfers between devices: 38.4 us -> none  [the longest x7 19.2 us: extended(): lax.ppermute(lax.slice_in_dim(block, block.shape[dim] - width, None, axis...]
    pallas_call x0 -> x1, Pallas kernels: none -> 36.9 us  [per_device(): pl.pallas_call(functools.partial(kernel, (cams, depth, slots, sub, tile,...]
    ppermute x14 -> x0, starting transfers between devices: 30.2 us -> none  [the longest x7 20.9 us: extended(): lax.ppermute(lax.slice_in_dim(block, block.shape[dim] - width, None, axis...]
    add x9 -> x0, other arithmetic: 16.4 us -> none  [the longest x3 9.62 us: binomial(): 0.25 * padded_depth[:-2] + 0.5 * padded_depth[1:-1]]
    dot_general x4 -> x0, matrix products: 12.7 us -> none  [per_device(): jnp.einsum('zksx,zksy->zxy', masked, chosen, preferred_element_type=jnp.f...]
    concatenate x4 -> x0, local copies, waits for them, and re-layouts: 8.17 us -> none  [extended(): block = jnp.concatenate([low, block, high], axis=dim)]
    gather x4 -> x0, local copies, waits for them, and re-layouts: 7.37 us -> none  [per_device(): chosen = stacked[crossings[camera, :, 0, :]]]
    unnamed x6 -> x1, local copies, waits for them, and re-layouts: 0.11 us -> 3.16 us
  transfers between devices with their start and end apart: 14 -> 0, of which waited for: 10 -> 0; matrix products, arithmetic and copies ran while one was open for 2% -> 0% of each run, Pallas kernels for 0% -> 0%
where the time goes in v1:
time: 40.2 us; the launch traced here: 40 us
  Pallas kernels  36.9 us (92%)
  local copies, waits for them, and re-layouts  3.16 us (8%)
    pallas_call x1, Pallas kernels, per_device(): pl.pallas_call(functools.partial(kernel, (cams, depth, slots, sub, tile,...  36.9 us
    unnamed x1, local copies, waits for them, and re-layouts  3.16 us

profile of v1, /device:TPU:0, one launch (start us, length us, event | category | flops | bytes accessed | tf_op | source)
XLA Modules:
  0.0 40.0 jit_solution(16574091333761713766)
XLA Ops:
  0.0 36.9 %shard_map.46 = f32[4,128,1024]{2,1,0:T(8,128)} custom-call(s32[4,3,1,4]{3,2,1,0:T(1,128)} %bitcast.4, s32[4,1,4]{2,1,0:T(1,128)} %bitcast.5, bf16[4,128,1024]{2,1,0:T(8,128)(2,1)} %images.1, bf16[4,4,3,64,128]{4,3,2,1,0:T(8,128)(2,1)} %weights.1), custom_call_target="tpu_custom_call" | custom-call | tf_op jit(solution)/shard_map/pallas_call | solution.py:240
  36.9 3.2 %copy.7 = f32[4,128,1024]{2,1,0:T(8,128)} copy(f32[4,128,1024]{2,1,0:T(8,128)} %shard_map.46) | data formatting | bytes 4194304

commit v2 on v1

--- a/solution.py
+++ b/solution.py
@@ -185,11 +185,11 @@
         both(functools.partial(halo_copy, j), "start", None)
         for z in range(depth):
             rows = pl.ds(z * tile, tile)
-            done[j % 2, rows, :] = dot(along[...], part[0, rows, :]) + dot(along[...], part[1, rows, :])
+            done[j, rows, :] = dot(along[...], part[0, rows, :]) + dot(along[...], part[1, rows, :])
 
     def finish_x(j):
         both(functools.partial(halo_copy, j), None, "recv")
-        high, low = split(done[j % 2] + dot(beside[...], inbox[j]))
+        high, low = split(done[j] + dot(beside[...], inbox[j]))
         cut = pl.ds(pl.multiple_of(offset(j) + LANES, LANES), width)
         field[0, :, cut] = high
         field[1, :, cut] = low
@@ -214,14 +214,12 @@
 
     for j in range(CHUNKS):
         project(j)
+    for j in range(CHUNKS):
+        finish_x(j)
+        if j == 0:
+            seam.start()
         if j >= 1:
-            finish_x(j - 1)
-            if j == 1:
-                seam.start()
-        if j >= 2:
-            finish_y(j - 2)
-    finish_x(CHUNKS - 1)
-    finish_y(CHUNKS - 2)
+            finish_y(j - 1)
     finish_y(CHUNKS - 1)
     for j in range(CHUNKS):
         both(functools.partial(image_copy, j), "send", None)
@@ -249,7 +247,7 @@
             pltpu.VMEM((rows, width), F32),
             pltpu.VMEM((2, rows, width), BF),
             pltpu.VMEM((2, rows, cols + 2 * LANES), BF),
-            pltpu.VMEM((2, rows, width), F32),
+            pltpu.VMEM((CHUNKS, rows, width), F32),
             pltpu.VMEM((CHUNKS, depth, tile, width), F32),
             pltpu.VMEM((width + 2 * LANES, width), BF),
             pltpu.VMEM((tile, tile), BF),

time: 40.2 us -> 37.6 us (0.935)
  Pallas kernels: 36.9 us -> 34.2 us
    pallas_call x1, Pallas kernels: 36.9 us -> 34.2 us  [per_device(): pl.pallas_call(functools.partial(kernel, (cams, depth, slots, sub, tile,...]
where the time goes in v2:
time: 37.6 us; the launch traced here: 37.4 us
  Pallas kernels  34.2 us (91%)
  local copies, waits for them, and re-layouts  3.16 us (8%)
    pallas_call x1, Pallas kernels, per_device(): pl.pallas_call(functools.partial(kernel, (cams, depth, slots, sub, tile,...  34.2 us
    unnamed x1, local copies, waits for them, and re-layouts  3.16 us

profile of v2, /device:TPU:0, one launch (start us, length us, event | category | flops | bytes accessed | tf_op | source)
XLA Modules:
  0.0 37.4 jit_solution(12448468714135380099)
XLA Ops:
  0.0 34.2 %shard_map.46 = f32[4,128,1024]{2,1,0:T(8,128)} custom-call(s32[4,3,1,4]{3,2,1,0:T(1,128)} %bitcast.4, s32[4,1,4]{2,1,0:T(1,128)} %bitcast.5, bf16[4,128,1024]{2,1,0:T(8,128)(2,1)} %images.1, bf16[4,4,3,64,128]{4,3,2,1,0:T(8,128)(2,1)} %weights.1), custom_call_target="tpu_custom_call" | custom-call | tf_op jit(solution)/shard_map/pallas_call | solution.py:238
  34.2 3.2 %copy.7 = f32[4,128,1024]{2,1,0:T(8,128)} copy(f32[4,128,1024]{2,1,0:T(8,128)} %shard_map.46) | data formatting | bytes 4194304

commit v3 on v2

--- a/solution.py
+++ b/solution.py
@@ -163,6 +163,12 @@
 
     layers = layer_matrix(depth)
 
+    def put(j, rows, value):
+        high, low = split(value)
+        cut = pl.ds(pl.multiple_of(offset(j) + LANES, LANES), width)
+        field[0, rows, cut] = high
+        field[1, rows, cut] = low
+
     def project(j):
         cut = pl.ds(offset(j), width)
         both(functools.partial(image_copy, j), None, "recv")
@@ -186,13 +192,14 @@
         for z in range(depth):
             rows = pl.ds(z * tile, tile)
             done[j, rows, :] = dot(along[...], part[0, rows, :]) + dot(along[...], part[1, rows, :])
+        put(j, pl.ds(0, depth * tile), done[j])
 
     def finish_x(j):
         both(functools.partial(halo_copy, j), None, "recv")
-        high, low = split(done[j] + dot(beside[...], inbox[j]))
-        cut = pl.ds(pl.multiple_of(offset(j) + LANES, LANES), width)
-        field[0, :, cut] = high
-        field[1, :, cut] = low
+        for z in range(depth):
+            for start in (0, tile - 16):
+                rows = pl.ds(z * tile + start, 16)
+                put(j, rows, done[j, rows, :] + dot(beside[rows, :], inbox[j]))
 
     mine = pl.multiple_of(jnp.where(gy == 0, cols, LANES), LANES)
     theirs = pl.multiple_of(jnp.where(gy == 0, 0, cols + LANES), LANES)

time: 37.6 us -> 37.5 us (level)
  no operation moved by 1% of the time
where the time goes in v3:
time: 37.5 us; the launch traced here: 37.3 us
  Pallas kernels  34.1 us (91%)
  local copies, waits for them, and re-layouts  3.16 us (8%)
    pallas_call x1, Pallas kernels, per_device(): pl.pallas_call(functools.partial(kernel, (cams, depth, slots, sub, tile,...  34.1 us
    unnamed x1, local copies, waits for them, and re-layouts  3.16 us

profile of v3, /device:TPU:0, one launch (start us, length us, event | category | flops | bytes accessed | tf_op | source)
XLA Modules:
  0.0 37.3 jit_solution(7122952387835979359)
XLA Ops:
  0.0 34.1 %shard_map.46 = f32[4,128,1024]{2,1,0:T(8,128)} custom-call(s32[4,3,1,4]{3,2,1,0:T(1,128)} %bitcast.4, s32[4,1,4]{2,1,0:T(1,128)} %bitcast.5, bf16[4,128,1024]{2,1,0:T(8,128)(2,1)} %images.1, bf16[4,4,3,64,128]{4,3,2,1,0:T(8,128)(2,1)} %weights.1), custom_call_target="tpu_custom_call" | custom-call | tf_op jit(solution)/shard_map/pallas_call | solution.py:245
  34.1 3.2 %copy.7 = f32[4,128,1024]{2,1,0:T(8,128)} copy(f32[4,128,1024]{2,1,0:T(8,128)} %shard_map.46) | data formatting | bytes 4194304
